TPU v7x, 32 devices: a whole 2x2x4 slice. The times are simulated.
32 devices in a mesh: groups: 2 (over y), ctx: 4 (over z), mp: 4 (over x, core).
Axes of the slice: x: 2, y: 2, z: 4, core: 2. Of those that a mesh axis runs over, the one named last changes fastest.
Arguments:
- query: bfloat16 [4096, 8192], P(('groups', 'ctx'), 'mp'), parts along dimension 0, may hold values from -200 to 200
- span_keys: bfloat16 [4096, 1024], P(('groups', 'ctx'), 'mp'), parts along dimension 0, may hold values from -6 to 6
- span_values: bfloat16 [4096, 1024], P(('groups', 'ctx'), 'mp'), parts along dimension 0, may hold values from -6 to 6
- cache_keys: bfloat16 [8192, 1024], P(('groups', 'ctx'), 'mp'), parts along dimension 0, may hold values from -13 to 13
- stored_values: bfloat16 [8192, 1024], P(('groups', 'ctx'), 'mp'), parts along dimension 0, may hold values from -6 to 6
- selected: int32 [8, 8, 2], P(('groups', 'ctx'), 'mp'), parts along dimension 0, may hold values from 0 to 7, as said below
Outputs:
- attended: bfloat16 [4096, 8192], P(('groups', 'ctx'), 'mp'), parts along dimension 0
There are 2 independent parts, one for each index of `groups`. A program takes and returns all parts, laid end to end along the dimension named above; each array names one. Nothing has to cross between parts.
Inputs may be any that keep to these rules, and one draw needn't show every extreme that they name: `selected`: the two blocks chosen for a query block and key head lie in different ranges of 2 consecutive blocks, starting at multiples of 2.
All inputs are finite; a program needn't handle non-finite values.
Results may differ from a plain program's by a relative error of at most 0.0047.
Values may be sent and summed in bfloat16 or wider, within the bound.
A program may use at most 64 MiB of HBM per device.

v0:
```python
import jax
import jax.numpy as jnp
from jax import lax
from jax.sharding import PartitionSpec as P

QUERY_HEADS = 64
KEY_VALUE_HEADS = 8
HEAD_DIMENSION = 128


def attend(query_group, all_keys, all_values, query_group_count):
    block_rows = query_group.shape[0]
    head_size = all_keys.shape[1]
    score_scale = head_size ** (-0.5)
    query_pos = jnp.arange(block_rows, dtype=jnp.int32)[:, None]
    key_pos = jnp.arange(all_keys.shape[0], dtype=jnp.int32)[None, :]
    visible = (key_pos >= block_rows) | (key_pos <= query_pos)
    results = []
    for member in range(query_group_count):
        query_head = query_group[:, member * head_size : (member + 1) * head_size]
        scores = jnp.dot(query_head, all_keys.T, preferred_element_type=jnp.float32) * score_scale
        scores = jnp.where(visible, scores, jnp.float32(-1e30))
        maxima = jnp.max(scores, axis=1, keepdims=True)
        exponent = jnp.exp(scores - maxima)
        denominator = jnp.sum(exponent, axis=1, keepdims=True)
        weights = (exponent / denominator).astype(jnp.bfloat16)
        results.append(
            jnp.dot(weights, all_values, preferred_element_type=jnp.float32).astype(jnp.bfloat16)
        )
    return jnp.concatenate(results, axis=1)


def per_device(query, span_keys, span_values, cache_keys, stored_values, selected):
    block_rows = query.shape[0]
    head_size = HEAD_DIMENSION
    kv_local = span_keys.shape[1] // head_size
    query_group_count = QUERY_HEADS // KEY_VALUE_HEADS
    wanted = selected[0]
    initial = jnp.zeros((kv_local, 2, block_rows, 2 * head_size), jnp.bfloat16)
    begin_row = jnp.int32(0)
    key_piece = lax.all_gather(cache_keys, "ctx", axis=0, tiled=True)
    value_piece = lax.all_gather(stored_values, "ctx", axis=0, tiled=True)
    piece_rows = key_piece.shape[0]
    updated = initial
    for collect_key_value_head in range(kv_local):
        for slot_index in range(2):
            first_row = wanted[collect_key_value_head, slot_index] * block_rows
            inside = (first_row >= begin_row) & (first_row < begin_row + piece_rows)
            offset = jnp.clip(first_row, 0, piece_rows - block_rows)
            key_tile = lax.dynamic_slice(
                key_piece,
                (offset, jnp.int32(collect_key_value_head * head_size)),
                (block_rows, head_size),
            )
            value_tile = lax.dynamic_slice(
                value_piece,
                (offset, jnp.int32(collect_key_value_head * head_size)),
                (block_rows, head_size),
            )
            tile_block = jnp.concatenate([key_tile, value_tile], axis=1)
            updated = updated.at[collect_key_value_head, slot_index].set(
                jnp.where(inside, tile_block, updated[collect_key_value_head, slot_index])
            )
    results = []
    for key_value_head in range(kv_local):
        query_group = query[
            :,
            key_value_head
            * query_group_count
            * head_size : (key_value_head + 1)
            * query_group_count
            * head_size,
        ]
        all_keys = jnp.concatenate(
            [
                span_keys[:, key_value_head * head_size : (key_value_head + 1) * head_size],
                updated[key_value_head, 0, :, :head_size],
                updated[key_value_head, 1, :, :head_size],
            ],
            axis=0,
        )
        all_values = jnp.concatenate(
            [
                span_values[:, key_value_head * head_size : (key_value_head + 1) * head_size],
                updated[key_value_head, 0, :, head_size:],
                updated[key_value_head, 1, :, head_size:],
            ],
            axis=0,
        )
        results.append(attend(query_group, all_keys, all_values, query_group_count))
    return jnp.concatenate(results, axis=1)


def solution(mesh):
    in_specs = (
        P(("groups", "ctx"), "mp"),
        P(("groups", "ctx"), "mp"),
        P(("groups", "ctx"), "mp"),
        P(("groups", "ctx"), "mp"),
        P(("groups", "ctx"), "mp"),
        P(("groups", "ctx"), "mp", None),
    )
    out_specs = P(("groups", "ctx"), "mp")
    return jax.shard_map(
        per_device, mesh=mesh, in_specs=in_specs, out_specs=out_specs, check_vma=False
    )
```

profile of v0, /device:TPU:0, one launch (start us, length us, event | category | flops | bytes accessed | tf_op | source)
XLA Modules:
  0.0 166.1 jit_solution(3036520839376949744)
XLA Ops:
  6.5 0.7 all-gather.5.cloned.1.call-update
  8.0 1.4 fusion.116
  12.7 1.0 fusion.115
  13.7 1.0 fusion.114
  14.7 42.9 %all-gather.5.cloned.1.call-done = bf16[4096,256]{1,0:T(8,128)(2,1)} async-done(((bf16[1024,256]{1,0:T(8,128)(2,1)}), bf16[4096,256]{1,0:T(8,128)(2,1)}) %all-gather.5.cloned.1.call-update) | async-done | bytes 2097168 | tf_op jit(solution)/shard_map/all_gather | solution.py:42
  57.6 1.2 dynamic-slice_bitcast_fusion.2
  58.8 45.0 %all-gather.3.cloned.1.call-done = bf16[4096,256]{1,0:T(8,128)(2,1)} async-done(((bf16[1024,256]{1,0:T(8,128)(2,1)}), bf16[4096,256]{1,0:T(8,128)(2,1)}) %all-gather.3.cloned.1.call-update) | async-done | bytes 2097168 | tf_op jit(solution)/shard_map/all_gather | solution.py:41
  103.9 1.2 dynamic-slice_bitcast_fusion.3
  105.2 1.3 fusion.97
  106.5 0.8 slice_bitcast_fusion.5
  107.3 5.6 %fusion.118 = (f32[512]{0:T(512)}, f32[512,1536]{0,1:T(8,128)}) fusion(bf16[512,2048]{1,0:T(8,128)(2,1)} %param.14, bf16[512,128]{1,0:T(8,128)(2,1)S(1)} %get-tuple-element.65, bf16[512,128]{1,0:T(8,128)(2,1)S(1)} %get-tuple-element.66, bf16[512,128]{1,0:T(8,128)(2,1)S(1)} %get-tuple-element.74, pred[1536]{0:T(1024)(128)(4,1)S(1)} %iota_compare_fusion.1), kind=kOutput, calls=%fused_computation.192 | convolution fusion | flops 206437888 | bytes 3673600 | tf_op jit(solution)/shard_map/dot_general | solution.py:21
  112.9 1.2 fusion.119
  114.1 1.2 fusion.120
  115.2 1.2 fusion.121
  116.4 1.2 fusion.122
  117.6 1.2 fusion.123
  118.8 1.2 fusion.124
  120.9 1.2 fusion.126
  122.1 1.2 fusion.127
  123.3 1.2 fusion.128
  124.5 1.2 fusion.129
  127.6 1.3 fusion.133
  128.9 3.0 %fusion.33 = f32[512]{0:T(512)} fusion(f32[512,1536]{0,1:T(8,128)} %get-tuple-element.82, f32[512]{0:T(512)} %get-tuple-element.81), kind=kLoop, calls=%fused_computation.82 | loop fusion | flops 1572352 | bytes 3149824 | tf_op jit(solution)/shard_map/reduce_sum | solution.py:25
  131.9 1.8 %fusion.34 = f32[512]{0:T(512)} fusion(f32[512,1536]{0,1:T(8,128)S(1)} %get-tuple-element.84, f32[512]{0:T(512)} %get-tuple-element.83), kind=kLoop, calls=%fused_computation.83 | loop fusion | flops 1572352 | bytes 3149824 | tf_op jit(solution)/shard_map/reduce_sum | solution.py:25
  133.7 3.3 %fusion.81 = bf16[512,2048]{0,1:T(8,128)(2,1)} fusion(f32[512,1536]{0,1:T(8,128)} %get-tuple-element.82, f32[512]{0:T(512)} %fusion.33, f32[512]{0:T(512)} %get-tuple-element.81, bf16[512,128]{1,0:T(8,128)(2,1)S(1)} %copy-done.2, bf16[512,128]{1,0:T(8,128)(2,1)S(1)} %copy-done.1, bf16[512,128]{1,0:T(8,128)(2,1)S(1)} %get-tuple-element.68), kind=kOutput, calls=%fused_computation.130 | convolution fusion | flops 204931072 | bytes 3674112 | tf_op jit(solution)/shard_map/dot_general | solution.py:28
  137.0 1.3 fusion.82
  138.3 1.3 fusion.35
  139.9 0.9 fusion.83
  146.2 0.7 fusion.88
  148.8 0.7 fusion.90
  153.1 0.8 fusion.46
  156.9 2.4 %copy.7 = bf16[512,2048]{1,0:T(8,128)(2,1)} copy(bf16[512,2048]{0,1:T(8,128)(2,1)S(1)} %fusion.96) | data formatting | bytes 4194304 | tf_op jit(solution)/shard_map/concatenate | solution.py:91
  (69 shorter events, 18.3 us)
Async XLA Ops:
  6.5 51.1 %all-gather.5.cloned.1.call-start = ((), (), s32[]{:S(2)}) async-start(), calls=%async_computation.1 | async-start | bytes 2621440 | tf_op jit(solution)/shard_map/all_gather | solution.py:42
  7.3 96.6 %all-gather.3.cloned.1.call-start = ((), (), s32[]{:S(2)}) async-start(), calls=%async_computation | async-start | bytes 2621440 | tf_op jit(solution)/shard_map/all_gather | solution.py:41
  12.1 114.9 %copy-start.14 = (pred[1536]{0:T(1024)(128)(4,1)}, pred[1536]{0:T(1024)(128)(4,1)S(1)}, u32[]{:S(2)}) copy-start(pred[1536]{0:T(1024)(128)(4,1)S(1)} %iota_compare_fusion.1) | copy-start | bytes 4612
  106.5 6.4 %copy-start.15 = (bf16[512,2048]{1,0:T(8,128)(2,1)S(1)}, bf16[512,2048]{1,0:T(8,128)(2,1)}, u32[]{:S(2)}) copy-start(bf16[512,2048]{1,0:T(8,128)(2,1)} %param.14) | copy-start | bytes 6291460
  128.9 4.8 %copy-start.1 = (bf16[512,128]{1,0:T(8,128)(2,1)S(1)}, bf16[512,128]{1,0:T(8,128)(2,1)}, u32[]{:S(2)}) copy-start(bf16[512,128]{1,0:T(8,128)(2,1)} %get-tuple-element.63) | copy-start | bytes 393220
  128.9 4.8 %copy-start.2 = (bf16[512,128]{1,0:T(8,128)(2,1)S(1)}, bf16[512,128]{1,0:T(8,128)(2,1)}, u32[]{:S(2)}) copy-start(bf16[512,128]{1,0:T(8,128)(2,1)} %get-tuple-element.64) | copy-start | bytes 393220
  133.7 3.3 %copy-start.12 = (f32[512]{0:T(512)S(1)}, f32[512]{0:T(512)}, u32[]{:S(2)}) copy-start(f32[512]{0:T(512)} %get-tuple-element.83) | copy-start | bytes 6148
  133.7 3.3 %copy-start.13 = (f32[512]{0:T(512)S(1)}, f32[512]{0:T(512)}, u32[]{:S(2)}) copy-start(f32[512]{0:T(512)} %fusion.34) | copy-start | bytes 6148
  138.3 1.6 copy-start
  138.3 1.6 copy-start.11
  139.9 0.9 copy-start.10
  141.3 0.7 copy-start.8
  142.5 0.7 copy-start.6
  143.7 0.7 copy-start.4
  146.2 0.7 copy-start.9
  146.9 0.7 copy-start.7
  148.7 0.7 copy-start.5
  150.0 0.7 copy-start.3
Sparse Core Ops, SparseCore 0:
  8.9 48.6 all-gather.4
  59.2 44.6 all-gather.2
where the time goes:
time: 167 us; the launch traced here: 166 us
  waiting for transfers between devices  89.3 us (53%)
  matrix products  35.8 us (21%)
  between operations  16.3 us (10%)
  other arithmetic  14.2 us (9%)
  local copies, waits for them, and re-layouts  10.4 us (6%)
    all_gather x1, waiting for transfers between devices, per_device(): key_piece = lax.all_gather(cache_keys, 'ctx', axis=0, tiled=True)  45 us
    all_gather x1, waiting for transfers between devices, per_device(): value_piece = lax.all_gather(stored_values, 'ctx', axis=0, tiled=True)  42.9 us
    dot_general x16, matrix products, attend(): jnp.dot(query_head, all_keys.T, preferred_element_type=jnp.float32)  21.3 us
    dot_general x16, matrix products, attend(): jnp.dot(weights, all_values, preferred_element_type=jnp.float32)  14.5 us
    reduce_sum x16, other arithmetic, attend(): denominator = jnp.sum(exponent, axis=1, keepdims=True)  12.8 us
  transfers between devices with their start and end apart: 2, of which 2 were waited for; matrix products, arithmetic and copies ran while one was open for 3% of the time, Pallas kernels for 0%

commit v1 on v0

v1 whole, which is shorter than its diff:
```python
import functools
import math

import jax
import jax.numpy as jnp
from jax import lax
from jax.experimental import pallas as pl
from jax.experimental.pallas import tpu as pltpu
from jax.sharding import PartitionSpec as P

QUERY_HEADS = 64
KEY_VALUE_HEADS = 8
HEAD = 128
GROUP = QUERY_HEADS // KEY_VALUE_HEADS
MESH = pl.DeviceIdType.MESH
CHUNK = 256


def partners(me, n):
    found = []
    if n & (n - 1) == 0:
        for t in range(n - 1, 0, -1):
            other = me
            for bit in range(n.bit_length()):
                if t >> bit & 1:
                    other = other + (1 << bit) * (1 - 2 * ((me // (1 << bit)) % 2))
            found.append((other, other))
    else:
        for t in range(1, n):
            found.append(((me + t) % n, (me + n - t) % n))
    return found


def kernel(n, kv, sel, query, span_keys, span_values, cache_keys, stored_values, out,
           qv, skv, svv, ckv, cvv, ov, all_sel, send, early, last, wide, acc, top,
           in_sem, out_sem, sel_send, sel_recv, send_sem, recv_sem):
    block = skv.shape[0]
    per_owner = ckv.shape[0] // block
    scale = HEAD ** (-0.5) * math.log2(math.e)
    me = lax.axis_index("ctx")
    others = partners(me, n)

    loads = [
        pltpu.make_async_copy(a, b, in_sem.at[i])
        for i, (a, b) in enumerate([
            (cache_keys, ckv), (stored_values, cvv), (query, qv),
            (span_keys, skv), (span_values, svv),
        ])
    ]
    for copy in loads:
        copy.start()

    barrier = pltpu.get_barrier_semaphore()
    for target, _ in others:
        pl.semaphore_signal(barrier, inc=1, device_id={"ctx": target}, device_id_type=MESH)
    pl.semaphore_wait(barrier, n - 1)

    sel_copies = []
    for j, (target, _) in enumerate(others):
        copy = pltpu.make_async_remote_copy(
            src_ref=sel, dst_ref=all_sel.at[j], send_sem=sel_send.at[j],
            recv_sem=sel_recv.at[j], device_id={"ctx": target}, device_id_type=MESH)
        copy.start()
        sel_copies.append(copy)

    def cols(h):
        return slice(h * HEAD, (h + 1) * HEAD)

    loads[0].wait()
    loads[1].wait()
    for copy in sel_copies:
        copy.wait()

    def held(first, second, cache, h):
        begin = me * per_owner
        found = cache[:block, cols(h)]
        for i in range(1, per_owner):
            wanted = (first == begin + i) | (second == begin + i)
            piece = cache[i * block:(i + 1) * block, cols(h)]
            found = jnp.where(jnp.full(found.shape, wanted), piece, found)
        return found

    remote = {}
    for h in range(kv):
        for j, (target, _) in enumerate(others):
            first, second = all_sel[j, 0, h, 0], all_sel[j, 0, h, 1]
            for kind, cache in enumerate((ckv, cvv)):
                send[h, j, kind] = held(first, second, cache, h)
                place = early[2 * h + kind].at[j + 1] if j < n - 2 else last[2 * h + kind]
                copy = pltpu.make_async_remote_copy(
                    src_ref=send.at[h, j, kind], dst_ref=place,
                    send_sem=send_sem.at[h, j, kind], recv_sem=recv_sem.at[h, j, kind],
                    device_id={"ctx": target}, device_id_type=MESH)
                copy.start()
                remote[h, j, kind] = copy
    for h in range(kv):
        for kind, cache in enumerate((ckv, cvv)):
            early[2 * h + kind][0] = held(sel[0, h, 0], sel[0, h, 1], cache, h)

    for copy in loads[2:]:
        copy.wait()
    wide[:, HEAD:] = jnp.ones((block, HEAD), jnp.bfloat16)

    def scores(rows, head, keys):
        return lax.dot_general(
            qv[rows, pl.ds(pl.multiple_of(head * HEAD, HEAD), HEAD)], keys,
            (((1,), (1,)), ((), ())), preferred_element_type=jnp.float32)

    def own(h):
        wide[:, :HEAD] = svv[:, cols(h)]

        @pl.loop(0, GROUP)
        def _(member):
            head = h * GROUP + member
            for start in range(0, block, CHUNK):
                rows, seen = slice(start, start + CHUNK), start + CHUNK
                s = scores(rows, head, skv[:seen, cols(h)])
                at = lax.broadcasted_iota(jnp.int32, (CHUNK, seen), 0) + start
                key = lax.broadcasted_iota(jnp.int32, (CHUNK, seen), 1)
                s = jnp.where(key <= at, s, -jnp.inf)
                m = jnp.max(s, axis=1, keepdims=True)
                p = jnp.exp2((s - m) * scale).astype(jnp.bfloat16)
                acc[head, rows] = jnp.dot(p, wide[:seen], preferred_element_type=jnp.float32)
                top[head, rows] = jnp.broadcast_to(m, (CHUNK, HEAD))

    def more(h, keys_ref, final):
        @pl.loop(0, GROUP)
        def _(member):
            head = h * GROUP + member
            for start in range(0, block, CHUNK):
                rows = slice(start, start + CHUNK)
                s = scores(rows, head, keys_ref[...])
                old = top[head, rows]
                m = jnp.maximum(old[:, :1], jnp.max(s, axis=1, keepdims=True))
                p = jnp.exp2((s - m) * scale).astype(jnp.bfloat16)
                shrink = jnp.exp2((old[:, :1] - m) * scale)
                total = acc[head, rows] * shrink + jnp.dot(
                    p, wide[...], preferred_element_type=jnp.float32)
                if final:
                    ov[rows, pl.ds(pl.multiple_of(head * HEAD, HEAD), HEAD)] = (
                        total[:, :HEAD] / total[:, HEAD:]).astype(jnp.bfloat16)
                else:
                    acc[head, rows] = total
                    top[head, rows] = jnp.broadcast_to(m, (CHUNK, HEAD))

    def owned(value, owner):
        begin = owner * per_owner
        return (value >= begin) & (value < begin + per_owner)

    def pick(tests, blocks):
        found = blocks[0][...]
        for test, other in zip(tests[1:], blocks[1:]):
            found = jnp.where(jnp.full(found.shape, test), other[...], found)
        return found

    owners = [me] + [source for _, source in others]
    for h in range(kv):
        own(h)
    stores = []
    for h in range(kv):
        first, second = sel[0, h, 0], sel[0, h, 1]
        swap = owned(first, owners[-1])
        one, two = jnp.where(swap, second, first), jnp.where(swap, first, second)
        for j in range(n - 2):
            for kind in range(2):
                remote[h, j, kind].wait_recv()
        picked_keys = skv.at[:, cols(h)]
        tests = [owned(one, owner) for owner in owners[:-1]]
        picked_keys[...] = pick(tests, [early[2 * h].at[i] for i in range(n - 1)])
        wide[:, :HEAD] = pick(tests, [early[2 * h + 1].at[i] for i in range(n - 1)])
        more(h, picked_keys, False)
        for kind in range(2):
            remote[h, n - 2, kind].wait_recv()
        tests = [owned(two, owner) for owner in owners]
        picked_keys[...] = pick(tests, [early[2 * h].at[i] for i in range(n - 1)] + [last[2 * h]])
        wide[:, :HEAD] = pick(
            tests, [early[2 * h + 1].at[i] for i in range(n - 1)] + [last[2 * h + 1]])
        more(h, picked_keys, True)
        columns = slice(h * GROUP * HEAD, (h + 1) * GROUP * HEAD)
        copy = pltpu.make_async_copy(ov.at[:, columns], out.at[:, columns], out_sem.at[h])
        copy.start()
        stores.append(copy)
    for copy in remote.values():
        copy.wait_send()
    for copy in stores:
        copy.wait()


def entry(n, kv, *refs):
    inputs, rest = refs[:7], list(refs[7:])
    head = rest[:8]
    rest = rest[8:]
    early, last, rest = rest[:2 * kv], rest[2 * kv:4 * kv], rest[4 * kv:]
    kernel(n, kv, *inputs, *head, early, last, *rest)


def per_device(n, query, span_keys, span_values, cache_keys, stored_values, selected):
    block, width = query.shape
    kv = span_keys.shape[1] // HEAD
    heads = width // HEAD
    bf, f32 = jnp.bfloat16, jnp.float32
    anywhere = pl.BlockSpec(memory_space=pl.ANY)
    dma = pltpu.SemaphoreType.DMA
    return pl.pallas_call(
        functools.partial(entry, n, kv),
        out_shape=jax.ShapeDtypeStruct(query.shape, bf),
        in_specs=[pl.BlockSpec(memory_space=pltpu.SMEM)] + [anywhere] * 5,
        out_specs=anywhere,
        scratch_shapes=[
            pltpu.VMEM(query.shape, bf),
            pltpu.VMEM(span_keys.shape, bf),
            pltpu.VMEM(span_values.shape, bf),
            pltpu.VMEM(cache_keys.shape, bf),
            pltpu.VMEM(stored_values.shape, bf),
            pltpu.VMEM(query.shape, bf),
            pltpu.SMEM((n - 1,) + selected.shape, jnp.int32),
            pltpu.VMEM((kv, n - 1, 2, block, HEAD), bf),
        ]
        + [pltpu.VMEM((n - 1, block, HEAD), bf)] * (2 * kv)
        + [pltpu.VMEM((block, HEAD), bf)] * (2 * kv)
        + [
            pltpu.VMEM((block, 2 * HEAD), bf),
            pltpu.VMEM((heads, block, 2 * HEAD), f32),
            pltpu.VMEM((heads, block, HEAD), f32),
            dma((5,)),
            dma((kv,)),
            dma((n - 1,)),
            dma((n - 1,)),
            dma((kv, n - 1, 2)),
            dma((kv, n - 1, 2)),
        ],
        compiler_params=pltpu.CompilerParams(
            collective_id=0, has_side_effects=True, vmem_limit_bytes=56 * 2**20),
        cost_estimate=pl.CostEstimate(
            flops=4 * block * 3 * block * width, bytes_accessed=6 * 2**20,
            transcendentals=heads * block * 3 * block),
    )(selected, query, span_keys, span_values, cache_keys, stored_values)


def solution(mesh):
    rows = P(("groups", "ctx"), "mp")
    return jax.shard_map(
        functools.partial(per_device, mesh.shape["ctx"]), mesh=mesh,
        in_specs=(rows,) * 5 + (P(("groups", "ctx"), "mp", None),),
        out_specs=rows, check_vma=False)
```

time: 167 us -> 79.1 us (0.47)
  waiting for transfers between devices: 89.3 us -> 0 us
  Pallas kernels: 0 us -> 75.8 us
  matrix products: 35.8 us -> 0 us
  between operations: 16.3 us -> 0.01 us
  other arithmetic: 14.2 us -> 0 us
  local copies, waits for them, and re-layouts: 10.4 us -> 3.16 us
    all_gather x2 -> x0, waiting for transfers between devices: 87.9 us -> none  [the longest x1 45 us: per_device(): key_piece = lax.all_gather(cache_keys, 'ctx', axis=0, tiled=True)]
    pallas_call x0 -> x1, Pallas kernels: none -> 75.8 us  [per_device(): pl.pallas_call(functools.partial(entry, n, kv), out_shape=jax.ShapeDtypeS...]
    dot_general x32 -> x0, matrix products: 35.8 us -> none  [the longest x16 21.3 us: attend(): jnp.dot(query_head, all_keys.T, preferred_element_type=jnp.float32)]
    reduce_sum x16 -> x0, other arithmetic: 12.8 us -> none  [attend(): denominator = jnp.sum(exponent, axis=1, keepdims=True)]
    concatenate x3 -> x0, local copies, waits for them, and re-layouts: 4.85 us -> none  [the longest x2 2.47 us: per_device(): tile_block = jnp.concatenate([key_tile, value_tile], axis=1)]
    slice x3 -> x0, local copies, waits for them, and re-layouts: 3.42 us -> none  [the longest x1 1.45 us: per_device(): first_row = wanted[collect_key_value_head, slot_index] * block_rows]
    unnamed x32 -> x1, local copies, waits for them, and re-layouts: 0.54 us -> 3.16 us
  transfers between devices with their start and end apart: 2 -> 0, of which waited for: 2 -> 0; matrix products, arithmetic and copies ran while one was open for 3% -> 0% of each run, Pallas kernels for 0% -> 0%
where the time goes in v1:
time: 79.1 us; the launch traced here: 78.9 us
  Pallas kernels  75.8 us (96%)
  local copies, waits for them, and re-layouts  3.16 us (4%)
    pallas_call x1, Pallas kernels, per_device(): pl.pallas_call(functools.partial(entry, n, kv), out_shape=jax.ShapeDtypeS...  75.8 us
    unnamed x1, local copies, waits for them, and re-layouts  3.16 us

profile of v1, /device:TPU:0, one launch (start us, length us, event | category | flops | bytes accessed | tf_op | source)
XLA Modules:
  0.0 78.9 jit_solution(5433089754095146258)
XLA Ops:
  0.0 75.8 %shard_map.64 = bf16[512,2048]{1,0:T(8,128)(2,1)} custom-call(s32[1,2,2]{2,1,0:T(2,128)} %refs_0_.1, bf16[512,2048]{1,0:T(8,128)(2,1)} %refs_1_.1, bf16[512,256]{1,0:T(8,128)(2,1)} %refs_2_.1, bf16[512,256]{1,0:T(8,128)(2,1)} %refs_3_.1, bf16[1024,256]{1,0:T(8,128)(2,1)} %refs_4_.1, bf16[1024,256]{1,0:T(8,128)(2,1)} %refs_5_.1), custom_call_target="tpu_custom_call" | custom-call | flops 6442450944 | bytes 6291456 | tf_op jit(solution)/shard_map/pallas_call | solution.py:204
  75.8 3.2 %copy.8 = bf16[512,2048]{1,0:T(8,128)(2,1)} copy(bf16[512,2048]{1,0:T(8,128)(2,1)} %shard_map.64) | data formatting | bytes 4194304

commit v2 on v1

--- a/solution.py
+++ b/solution.py
@@ -19,7 +19,8 @@
 def partners(me, n):
     found = []
     if n & (n - 1) == 0:
-        for t in range(n - 1, 0, -1):
+        order = [1, 3, 2] if n == 4 else range(n - 1, 0, -1)
+        for t in order:
             other = me
             for bit in range(n.bit_length()):
                 if t >> bit & 1:
@@ -31,8 +32,21 @@
     return found
 
 
+def sending(me, n, others):
+    steps = [(j, target) for j, (target, _) in enumerate(others)]
+    if n != 4:
+        return steps
+    inner = ((me + 1) % n) // 2
+    near, far = others[0][0], others[2][0]
+    return [
+        (2 - 2 * inner, inner * near + (1 - inner) * far),
+        steps[1],
+        (2 * inner, (1 - inner) * near + inner * far),
+    ]
+
+
 def kernel(n, kv, sel, query, span_keys, span_values, cache_keys, stored_values, out,
-           qv, skv, svv, ckv, cvv, ov, all_sel, send, early, last, wide, acc, top,
+           qv, skv, svv, ckv, cvv, ov, all_sel, send, got, wide, acc, top, probs,
            in_sem, out_sem, sel_send, sel_recv, send_sem, recv_sem):
     block = skv.shape[0]
     per_owner = ckv.shape[0] // block
@@ -80,22 +94,21 @@
             found = jnp.where(jnp.full(found.shape, wanted), piece, found)
         return found
 
-    remote = {}
-    for h in range(kv):
-        for j, (target, _) in enumerate(others):
+    def remote(h, j, kind, target):
+        return pltpu.make_async_remote_copy(
+            src_ref=send.at[h, j, kind], dst_ref=got.at[h, j, kind],
+            send_sem=send_sem.at[h, j, kind], recv_sem=recv_sem.at[h, j, kind],
+            device_id={"ctx": target}, device_id_type=MESH)
+
+    for h in range(kv):
+        for j, target in sending(me, n, others):
             first, second = all_sel[j, 0, h, 0], all_sel[j, 0, h, 1]
             for kind, cache in enumerate((ckv, cvv)):
                 send[h, j, kind] = held(first, second, cache, h)
-                place = early[2 * h + kind].at[j + 1] if j < n - 2 else last[2 * h + kind]
-                copy = pltpu.make_async_remote_copy(
-                    src_ref=send.at[h, j, kind], dst_ref=place,
-                    send_sem=send_sem.at[h, j, kind], recv_sem=recv_sem.at[h, j, kind],
-                    device_id={"ctx": target}, device_id_type=MESH)
-                copy.start()
-                remote[h, j, kind] = copy
+                remote(h, j, kind, target).start()
     for h in range(kv):
         for kind, cache in enumerate((ckv, cvv)):
-            early[2 * h + kind][0] = held(sel[0, h, 0], sel[0, h, 1], cache, h)
+            got[h, n - 1, kind] = held(sel[0, h, 0], sel[0, h, 1], cache, h)
 
     for copy in loads[2:]:
         copy.wait()
@@ -143,55 +156,79 @@
                     acc[head, rows] = total
                     top[head, rows] = jnp.broadcast_to(m, (CHUNK, HEAD))
 
+    def weigh(h, keys_ref):
+        @pl.loop(0, GROUP)
+        def _(member):
+            head = h * GROUP + member
+            for start in range(0, block, CHUNK):
+                rows = slice(start, start + CHUNK)
+                s = scores(rows, head, keys_ref[...])
+                old = top[head, rows]
+                m = jnp.maximum(old[:, :1], jnp.max(s, axis=1, keepdims=True))
+                probs[member, rows] = jnp.exp2((s - m) * scale).astype(jnp.bfloat16)
+                acc[head, rows] = acc[head, rows] * jnp.exp2((old[:, :1] - m) * scale)
+
+    def finish(h):
+        @pl.loop(0, GROUP)
+        def _(member):
+            head = h * GROUP + member
+            for start in range(0, block, CHUNK):
+                rows = slice(start, start + CHUNK)
+                total = acc[head, rows] + jnp.dot(
+                    probs[member, rows], wide[...], preferred_element_type=jnp.float32)
+                ov[rows, pl.ds(pl.multiple_of(head * HEAD, HEAD), HEAD)] = (
+                    total[:, :HEAD] / total[:, HEAD:]).astype(jnp.bfloat16)
+
     def owned(value, owner):
         begin = owner * per_owner
         return (value >= begin) & (value < begin + per_owner)
 
-    def pick(tests, blocks):
-        found = blocks[0][...]
-        for test, other in zip(tests[1:], blocks[1:]):
-            found = jnp.where(jnp.full(found.shape, test), other[...], found)
+    sources = [source for _, source in others]
+
+    def pick(value, h, kind, slots):
+        found = got[h, n - 1, kind]
+        for j in slots:
+            test = jnp.full(found.shape, owned(value, sources[j]))
+            found = jnp.where(test, got[h, j, kind], found)
         return found
 
-    owners = [me] + [source for _, source in others]
+    def arrived(h, j, kind):
+        remote(h, j, kind, others[j][0]).wait_recv()
+
     for h in range(kv):
         own(h)
     stores = []
     for h in range(kv):
         first, second = sel[0, h, 0], sel[0, h, 1]
-        swap = owned(first, owners[-1])
+        swap = owned(first, sources[-1])
         one, two = jnp.where(swap, second, first), jnp.where(swap, first, second)
-        for j in range(n - 2):
-            for kind in range(2):
-                remote[h, j, kind].wait_recv()
-        picked_keys = skv.at[:, cols(h)]
-        tests = [owned(one, owner) for owner in owners[:-1]]
-        picked_keys[...] = pick(tests, [early[2 * h].at[i] for i in range(n - 1)])
-        wide[:, :HEAD] = pick(tests, [early[2 * h + 1].at[i] for i in range(n - 1)])
-        more(h, picked_keys, False)
+        picked = skv.at[:, cols(h)]
         for kind in range(2):
-            remote[h, n - 2, kind].wait_recv()
-        tests = [owned(two, owner) for owner in owners]
-        picked_keys[...] = pick(tests, [early[2 * h].at[i] for i in range(n - 1)] + [last[2 * h]])
-        wide[:, :HEAD] = pick(
-            tests, [early[2 * h + 1].at[i] for i in range(n - 1)] + [last[2 * h + 1]])
-        more(h, picked_keys, True)
+            for j in range(n - 2):
+                arrived(h, j, kind)
+        picked[...] = pick(one, h, 0, range(n - 2))
+        wide[:, :HEAD] = pick(one, h, 1, range(n - 2))
+        more(h, picked, False)
+        arrived(h, n - 2, 0)
+        picked[...] = pick(two, h, 0, range(n - 1))
+        if h == kv - 1:
+            weigh(h, picked)
+        arrived(h, n - 2, 1)
+        wide[:, :HEAD] = pick(two, h, 1, range(n - 1))
+        if h == kv - 1:
+            finish(h)
+        else:
+            more(h, picked, True)
         columns = slice(h * GROUP * HEAD, (h + 1) * GROUP * HEAD)
         copy = pltpu.make_async_copy(ov.at[:, columns], out.at[:, columns], out_sem.at[h])
         copy.start()
         stores.append(copy)
-    for copy in remote.values():
-        copy.wait_send()
+    for h in range(kv):
+        for j in range(n - 1):
+            for kind in range(2):
+                remote(h, j, kind, others[j][0]).wait_send()
     for copy in stores:
         copy.wait()
-
-
-def entry(n, kv, *refs):
-    inputs, rest = refs[:7], list(refs[7:])
-    head = rest[:8]
-    rest = rest[8:]
-    early, last, rest = rest[:2 * kv], rest[2 * kv:4 * kv], rest[4 * kv:]
-    kernel(n, kv, *inputs, *head, early, last, *rest)
 
 
 def per_device(n, query, span_keys, span_values, cache_keys, stored_values, selected):
@@ -202,7 +239,7 @@
     anywhere = pl.BlockSpec(memory_space=pl.ANY)
     dma = pltpu.SemaphoreType.DMA
     return pl.pallas_call(
-        functools.partial(entry, n, kv),
+        functools.partial(kernel, n, kv),
         out_shape=jax.ShapeDtypeStruct(query.shape, bf),
         in_specs=[pl.BlockSpec(memory_space=pltpu.SMEM)] + [anywhere] * 5,
         out_specs=anywhere,
@@ -215,13 +252,11 @@
             pltpu.VMEM(query.shape, bf),
             pltpu.SMEM((n - 1,) + selected.shape, jnp.int32),
             pltpu.VMEM((kv, n - 1, 2, block, HEAD), bf),
-        ]
-        + [pltpu.VMEM((n - 1, block, HEAD), bf)] * (2 * kv)
-        + [pltpu.VMEM((block, HEAD), bf)] * (2 * kv)
-        + [
+            pltpu.VMEM((kv, n, 2, block, HEAD), bf),
             pltpu.VMEM((block, 2 * HEAD), bf),
             pltpu.VMEM((heads, block, 2 * HEAD), f32),
             pltpu.VMEM((heads, block, HEAD), f32),
+            pltpu.VMEM((GROUP, block, block), bf),
             dma((5,)),
             dma((kv,)),
             dma((n - 1,)),
@@ -230,7 +265,7 @@
             dma((kv, n - 1, 2)),
         ],
         compiler_params=pltpu.CompilerParams(
-            collective_id=0, has_side_effects=True, vmem_limit_bytes=56 * 2**20),
+            collective_id=0, has_side_effects=True, vmem_limit_bytes=(28 + 8 * kv * n * block * HEAD // 2**20) * 2**20),
         cost_estimate=pl.CostEstimate(
             flops=4 * block * 3 * block * width, bytes_accessed=6 * 2**20,
             transcendentals=heads * block * 3 * block),

time: 79.1 us -> 77.2 us (0.976)
  Pallas kernels: 75.8 us -> 69.3 us
  local copies, waits for them, and re-layouts: 3.16 us -> 7.57 us
    pallas_call x1, Pallas kernels: 75.8 us -> 69.3 us  [per_device(): pl.pallas_call(functools.partial(kernel, n, kv), out_shape=jax.ShapeDtype...]
    unnamed x1 -> x13, local copies, waits for them, and re-layouts: 3.16 us -> 7.57 us
where the time goes in v2:
time: 77.2 us; the launch traced here: 76.9 us
  Pallas kernels  69.3 us (90%)
  local copies, waits for them, and re-layouts  7.57 us (10%)
    pallas_call x1, Pallas kernels, per_device(): pl.pallas_call(functools.partial(kernel, n, kv), out_shape=jax.ShapeDtype...  69.3 us
    unnamed x13, local copies, waits for them, and re-layouts  7.57 us

profile of v2, /device:TPU:0, one launch (start us, length us, event | category | flops | bytes accessed | tf_op | source)
XLA Modules:
  0.0 76.9 jit_solution(3135495102491453028)
XLA Ops:
  0.0 0.0 copy-start
  0.0 1.6 %copy-done = bf16[512,2048]{1,0:T(8,128)(2,1)S(1)} copy-done((bf16[512,2048]{1,0:T(8,128)(2,1)S(1)}, bf16[512,2048]{1,0:T(8,128)(2,1)}, u32[]{:S(2)}) %copy-start) | copy-done | bytes 2097176
  1.6 0.0 copy-start.1
  1.6 1.0 %copy-done.1 = bf16[1024,256]{1,0:T(8,128)(2,1)S(1)} copy-done((bf16[1024,256]{1,0:T(8,128)(2,1)S(1)}, bf16[1024,256]{1,0:T(8,128)(2,1)}, u32[]{:S(2)}) %copy-start.1) | copy-done | bytes 524312
  2.6 0.0 copy-start.2
  2.6 1.0 %copy-done.2 = bf16[1024,256]{1,0:T(8,128)(2,1)S(1)} copy-done((bf16[1024,256]{1,0:T(8,128)(2,1)S(1)}, bf16[1024,256]{1,0:T(8,128)(2,1)}, u32[]{:S(2)}) %copy-start.2) | copy-done | bytes 524312
  3.7 0.0 copy-start.3
  3.7 0.9 %copy-done.3 = bf16[512,256]{1,0:T(8,128)(2,1)S(1)} copy-done((bf16[512,256]{1,0:T(8,128)(2,1)S(1)}, bf16[512,256]{1,0:T(8,128)(2,1)}, u32[]{:S(2)}) %copy-start.3) | copy-done | bytes 262168
  4.6 0.0 copy-start.4
  4.6 0.9 %copy-done.4 = bf16[512,256]{1,0:T(8,128)(2,1)S(1)} copy-done((bf16[512,256]{1,0:T(8,128)(2,1)S(1)}, bf16[512,256]{1,0:T(8,128)(2,1)}, u32[]{:S(2)}) %copy-start.4) | copy-done | bytes 262168
  5.6 0.0 copy-start.5
  5.6 0.7 copy-done.5
  6.3 69.3 %shard_map.64 = bf16[512,2048]{1,0:T(8,128)(2,1)S(1)} custom-call(s32[1,2,2]{2,1,0:T(2,128)S(1)} %copy-done.5, bf16[512,2048]{1,0:T(8,128)(2,1)S(1)} %copy-done, bf16[512,256]{1,0:T(8,128)(2,1)S(1)} %copy-done.3, bf16[512,256]{1,0:T(8,128)(2,1)S(1)} %copy-done.4, bf16[1024,256]{1,0:T(8,128)(2,1)S(1)} %copy-done.1, bf16[1024,256]{1,0:T(8,128)(2,1)S(1)} %copy-done.2), custom_call_target="tpu_custom_call" | custom-call | flops 6442450944 | bytes 6291456 | tf_op jit(solution)/shard_map/pallas_call | solution.py:241
  75.6 1.3 %copy.8 = bf16[512,2048]{1,0:T(8,128)(2,1)} copy(bf16[512,2048]{1,0:T(8,128)(2,1)S(1)} %shard_map.64) | data formatting | bytes 4194304
Async XLA Ops:
  0.0 1.6 %copy-start = (bf16[512,2048]{1,0:T(8,128)(2,1)S(1)}, bf16[512,2048]{1,0:T(8,128)(2,1)}, u32[]{:S(2)}) copy-start(bf16[512,2048]{1,0:T(8,128)(2,1)} %query.1) | copy-start | bytes 6291460
  1.6 1.0 %copy-start.1 = (bf16[1024,256]{1,0:T(8,128)(2,1)S(1)}, bf16[1024,256]{1,0:T(8,128)(2,1)}, u32[]{:S(2)}) copy-start(bf16[1024,256]{1,0:T(8,128)(2,1)} %cache_keys.1) | copy-start | bytes 1572868
  2.6 1.0 %copy-start.2 = (bf16[1024,256]{1,0:T(8,128)(2,1)S(1)}, bf16[1024,256]{1,0:T(8,128)(2,1)}, u32[]{:S(2)}) copy-start(bf16[1024,256]{1,0:T(8,128)(2,1)} %stored_values.1) | copy-start | bytes 1572868
  3.7 0.9 %copy-start.3 = (bf16[512,256]{1,0:T(8,128)(2,1)S(1)}, bf16[512,256]{1,0:T(8,128)(2,1)}, u32[]{:S(2)}) copy-start(bf16[512,256]{1,0:T(8,128)(2,1)} %span_keys.1) | copy-start | bytes 786436
  4.6 0.9 %copy-start.4 = (bf16[512,256]{1,0:T(8,128)(2,1)S(1)}, bf16[512,256]{1,0:T(8,128)(2,1)}, u32[]{:S(2)}) copy-start(bf16[512,256]{1,0:T(8,128)(2,1)} %span_values.1) | copy-start | bytes 786436
  5.6 0.7 copy-start.5
